TPU v7x, 512 devices: a whole 4x4x16 slice. The times are simulated.
512 devices in a mesh: dp: 16 (over y, x), expert: 32 (over z, core).
Axes of the slice: x: 4, y: 4, z: 16, core: 2. Of those that a mesh axis runs over, the one named last changes fastest.
Arguments:
- tokens: bfloat16 [32768, 2048], P(('dp', 'expert')), may hold values from -6 to 6
- route_ids: int32 [32768, 8], P(('dp', 'expert')), may hold values from 0 to 127, all different within a row; in each aligned block of 64 rows (0 to 63, 64 to 127, ...) at most 8 rows name the same one
- route_weights: bfloat16 [32768, 8], P(('dp', 'expert')), may hold values from 0.099609375 to 0.5
- placement: int32 [128], replicated, may hold values from 0 to 127, each once
- gate_proj: bfloat16 [16, 32, 1, 192, 2048], P('dp', 'expert'), may hold values from -0.125 to 0.125
- up_proj: bfloat16 [16, 32, 1, 192, 2048], P('dp', 'expert'), may hold values from -0.125 to 0.125
- down_proj: bfloat16 [16, 32, 1, 192, 2048], P('dp', 'expert'), may hold values from -0.21875 to 0.21875
Outputs:
- mixed: bfloat16 [32768, 2048], P(('dp', 'expert'))
Inputs may be any that keep to these rules, and one draw needn't show every extreme that they name: `route_ids`: the 8 ids of a token differ. Among the rows of one device no expert is named more than 8 times, and in every draw some expert is named exactly 8 times by the rows of some device. `placement`: each slot holds exactly one expert.
All inputs are finite; a program needn't handle non-finite values.
Results may differ from a plain program's by a relative error of at most 0.0058.
Values may be sent and summed in bfloat16 or wider, within the bound.
A program may use at most 128 MiB of HBM per device.

v0:
```python
import jax
import jax.numpy as jnp
from jax import lax
from jax.sharding import PartitionSpec as P

CAP = 8


def swapped(value, axis, stride):
    mask = 2**stride
    pairs = [(source, source ^ mask) for source in range(lax.axis_size(axis))]
    return lax.ppermute(value, axis, pairs)


def project(rows, gate_w, up_w, down_w):
    gate = jnp.einsum("bkcd,kfd->bkcf", rows, gate_w, preferred_element_type=jnp.float32)
    up = jnp.einsum("bkcd,kfd->bkcf", rows, up_w, preferred_element_type=jnp.float32)
    hidden = (jax.nn.silu(gate) * up).astype(jnp.bfloat16)
    return jnp.einsum("bkcf,kfd->bkcd", hidden, down_w, preferred_element_type=jnp.float32)


def on_device(tokens, route_ids, route_weights, placement, gate_proj, up_proj, down_proj):
    n_rows = lax.axis_size("dp")
    n_cols = lax.axis_size("expert")
    groups = n_cols // 4
    subsets = n_rows // 4
    per_slot = gate_proj.shape[2]
    width = tokens.shape[1]
    tok_count = tokens.shape[0]
    topk = route_ids.shape[1]
    experts = placement.shape[0]
    capacity = CAP
    expert_hot = (
        route_ids[:, :, None] == jnp.arange(experts, dtype=jnp.int32)[None, None, :]
    ).astype(jnp.int32)
    slot_ids = jnp.sum(expert_hot * placement[None, None, :], axis=2)
    flat_hot = expert_hot.reshape(tok_count * topk, experts)
    earlier = jnp.cumsum(flat_hot, axis=0) - flat_hot
    position = jnp.sum(earlier * flat_hot, axis=1).reshape(tok_count, topk)
    row_of = slot_ids // (groups * per_slot)
    group_of = slot_ids // per_slot % groups
    inner_of = slot_ids % per_slot
    target = (group_of * (n_rows * per_slot) + row_of * per_slot + inner_of) * capacity + position
    buffer_rows = experts * capacity
    lanes = jnp.arange(buffer_rows, dtype=jnp.int32)
    matches = target[None, :, :] == lanes[:, None, None]
    dispatch = jnp.sum(matches.astype(jnp.int32), axis=2).astype(jnp.bfloat16)
    outgoing = jnp.dot(dispatch, tokens, preferred_element_type=jnp.float32).astype(jnp.bfloat16)
    outgoing = outgoing.reshape(groups, n_rows * per_slot, capacity, width)
    by_rows = lax.all_to_all(outgoing, "dp", split_axis=1, concat_axis=1, tiled=True)
    by_rows = by_rows.reshape(n_cols, subsets * per_slot, capacity, width)
    arrived = lax.all_to_all(by_rows, "expert", split_axis=0, concat_axis=0, tiled=True)
    arrived = arrived.reshape(n_cols * subsets, per_slot, capacity, width)
    own_gate = gate_proj[0, 0]
    own_up = up_proj[0, 0]
    own_down = down_proj[0, 0]
    far_gate, far_up, far_down = swapped((own_gate, own_up, own_down), "expert", 1)
    gate_half = jnp.concatenate([own_gate, far_gate], axis=1)
    up_half = jnp.concatenate([own_up, far_up], axis=1)
    down_half = jnp.concatenate([own_down, far_down], axis=1)
    partner_rows = swapped(arrived, "expert", 0)
    partner_part = project(partner_rows, gate_half, up_half, down_half)
    returned = swapped(partner_part, "expert", 0)
    own_part = project(arrived, gate_half, up_half, down_half)
    result = (own_part + returned).astype(jnp.bfloat16)
    result = result.reshape(n_cols, subsets * per_slot, capacity, width)
    going_back = lax.all_to_all(result, "expert", split_axis=0, concat_axis=0, tiled=True)
    going_back = going_back.reshape(groups, n_rows * per_slot, capacity, width)
    at_home = lax.all_to_all(going_back, "dp", split_axis=1, concat_axis=1, tiled=True)
    flat_rows = at_home.reshape(buffer_rows, width)
    picked = target[:, :, None] == lanes[None, None, :]
    mixing = jnp.sum(
        jnp.where(picked, route_weights[:, :, None], jnp.zeros((), jnp.bfloat16)), axis=1
    )
    return jnp.dot(mixing, flat_rows, preferred_element_type=jnp.float32).astype(jnp.bfloat16)


def solution(mesh):
    in_specs = (
        P(("dp", "expert"), None),
        P(("dp", "expert"), None),
        P(("dp", "expert"), None),
        P(),
        P("dp", "expert", None, None, None),
        P("dp", "expert", None, None, None),
        P("dp", "expert", None, None, None),
    )
    out_specs = P(("dp", "expert"), None)
    return jax.shard_map(
        on_device, mesh=mesh, in_specs=in_specs, out_specs=out_specs, check_vma=False
    )
```

profile of v0, /device:TPU:6, one launch (start us, length us, event | category | flops | bytes accessed | tf_op | source)
XLA Modules:
  0.0 670.3 jit_solution(16818391591064527323)
XLA Ops:
  6.3 55.9 %all_to_all.20 = bf16[8,16,8,2048]{3,2,0,1:T(8,128)(2,1)S(1)} all-to-all(bf16[8,16,8,2048]{3,2,0,1:T(8,128)(2,1)S(1)} %copy.67), channel_id=1, replica_groups=mesh['dp'=16,'expert'=32] {'dp'}, dimensions={1} | all-to-all | bytes 8388608 | tf_op jit(solution)/shard_map/all_to_all | solution.py:50
  62.5 4.0 copy.69
  66.4 205.7 %all_to_all.21 = bf16[32,4,8,2048]{3,1,2,0:T(4,128)(2,1)S(1)} all-to-all(bf16[32,4,8,2048]{3,1,2,0:T(4,128)(2,1)S(1)} %copy.69), channel_id=1, replica_groups=mesh['dp'=16,'expert'=32] {'expert'}, dimensions={0} | all-to-all | bytes 8388608 | tf_op jit(solution)/shard_map/all_to_all | solution.py:52
  272.1 4.0 copy.70
  276.1 7.1 %reshape.159 = bf16[128,1,8,2048]{3,0,2,1:T(8,128)(2,1)} reshape(bf16[32,4,8,2048]{3,1,0,2:T(4,128)(2,1)} %copy.70) | data formatting | bytes 8388608 | tf_op jit(solution)/shard_map/reshape | solution.py:53
  287.0 3.9 collective-permute-start.2
  291.0 2.1 collective-permute-start
  293.1 14.2 %collective-permute-done.1 = bf16[1,192,2048]{2,1,0:T(8,128)(2,1)S(1)} collective-permute-done((bf16[1,192,2048]{2,1,0:T(8,128)(2,1)S(1)}, bf16[1,192,2048]{2,1,0:T(8,128)(2,1)S(1)}, u32[]{:S(2)}, u32[]{:S(2)}) %collective-permute-start.1) | collective-permute-done | bytes 786464 | tf_op jit(solution)/shard_map/ppermute | solution.py:12
  307.3 3.0 fusion.3
  310.4 13.8 %collective-permute-done.2 = bf16[1,192,2048]{2,1,0:T(8,128)(2,1)S(1)} collective-permute-done((bf16[1,192,2048]{2,1,0:T(8,128)(2,1)S(1)}, bf16[1,192,2048]{2,1,0:T(8,128)(2,1)S(1)}, u32[]{:S(2)}, u32[]{:S(2)}) %collective-permute-start.2) | collective-permute-done | bytes 786464 | tf_op jit(solution)/shard_map/ppermute | solution.py:12
  325.1 15.7 %collective-permute-done = bf16[1,192,2048]{2,1,0:T(8,128)(2,1)} collective-permute-done((bf16[1,192,2048]{2,1,0:T(8,128)(2,1)S(1)}, bf16[1,192,2048]{2,1,0:T(8,128)(2,1)}, u32[]{:S(2)}, u32[]{:S(2)}) %collective-permute-start) | collective-permute-done | bytes 786464 | tf_op jit(solution)/shard_map/ppermute | solution.py:12
  340.8 10.4 %convolution_bitcast_fusion = f32[128,1,8,2048]{3,0,2,1:T(8,128)} fusion(bf16[128,1,8,2048]{3,0,2,1:T(8,128)(2,1)} %copy-done.3, f32[384,128,8]{1,0,2:T(8,128)} %fusion.3, bf16[1,192,2048]{2,1,0:T(8,128)(2,1)} %copy-done.8, bf16[1,192,2048]{2,1,0:T(8,128)(2,1)S(1)} %bitcast.151, bf16[1,192,2048]{2,1,0:T(8,128)(2,1)} %collective-permute-done, ...), kind=kOutput, calls=%fused_computation.2 | convolution fusion | flops 3229876224 | bytes 17301504 | tf_op jit(solution)/shard_map/bkcf,kfd->bkcd/dot_general | solution.py:19
  353.1 6.9 %reshape.156 = bf16[128,8,2048]{2,0,1:T(8,128)(2,1)} reshape(bf16[32,4,8,2048]{3,1,0,2:T(4,128)(2,1)} %copy.70) | data formatting | bytes 8388608 | tf_op jit(solution)/shard_map/reshape.4
  360.0 5.4 fusion.24
  365.5 10.4 %fusion.20 = f32[2048,128,8]{0,1,2:T(8,128)} fusion(bf16[128,8,2048]{2,0,1:T(8,128)(2,1)} %reshape.156, f32[384,128,8]{1,0,2:T(8,128)} %fusion.24, bf16[1,192,2048]{2,1,0:T(8,128)(2,1)} %copy-done.8, bf16[1,192,2048]{2,1,0:T(8,128)(2,1)S(1)} %bitcast.152, bf16[1,192,2048]{2,1,0:T(8,128)(2,1)} %collective-permute-done, bf16[1,192,2048]{2,1,0:T(8,128)(2,1)S(1)} %bitcast.155), kind=kOutput, calls=%fused_computation.32 | convolution fusion | flops 3229876224 | bytes 17301504 | tf_op jit(solution)/shard_map/bkcf,kfd->bkcd/dot_general | solution.py:19
  375.9 9.1 %fusion = bf16[128,1,8,2048]{3,0,2,1:T(8,128)(2,1)} fusion(f32[128,1,8,2048]{3,0,2,1:T(8,128)} %collective-permute-done.4, f32[2048,128,8]{0,1,2:T(8,128)} %fusion.20), kind=kLoop, calls=%fused_computation.1 | loop fusion | flops 4194304 | bytes 20971520 | tf_op jit(solution)/shard_map/convert_element_type | solution.py:65
  385.1 7.2 %reshape.162 = bf16[32,4,8,2048]{3,1,0,2:T(4,128)(2,1)} reshape(bf16[128,1,8,2048]{3,0,2,1:T(8,128)(2,1)} %fusion) | data formatting | bytes 8388608 | tf_op jit(solution)/shard_map/reshape | solution.py:66
  392.2 4.3 copy.76
  396.5 194.4 %all_to_all.22 = bf16[32,4,8,2048]{3,1,2,0:T(4,128)(2,1)S(1)} all-to-all(bf16[32,4,8,2048]{3,1,2,0:T(4,128)(2,1)S(1)} %copy.76), channel_id=1, replica_groups=mesh['dp'=16,'expert'=32] {'expert'}, dimensions={0} | all-to-all | bytes 8388608 | tf_op jit(solution)/shard_map/all_to_all | solution.py:67
  590.9 4.4 copy.77
  595.3 2.3 copy.78
  597.5 7.1 %all-to-all-start.3 = ((bf16[8,16,8,2048]{3,2,0,1:T(8,128)(2,1)}), bf16[8,16,8,2048]{3,2,0,1:T(8,128)(2,1)}, u32[]{:S(2)}, u32[]{:S(2)}) async-start(bf16[8,16,8,2048]{3,2,0,1:T(8,128)(2,1)} %copy.78), calls=%async_computation.3 | async-start | bytes 8388608 | tf_op jit(solution)/shard_map/all_to_all | solution.py:69
  605.5 60.7 %all-to-all-done.3 = bf16[8,16,8,2048]{3,2,0,1:T(8,128)(2,1)} async-done(((bf16[8,16,8,2048]{3,2,0,1:T(8,128)(2,1)}), bf16[8,16,8,2048]{3,2,0,1:T(8,128)(2,1)}, u32[]{:S(2)}, u32[]{:S(2)}) %all-to-all-start.3) | async-done | bytes 4194336 | tf_op jit(solution)/shard_map/all_to_all | solution.py:69
  666.2 2.5 copy.79
  (45 shorter events, 15.5 us)
Async XLA Ops:
  0.0 4.4 copy-start
  276.1 9.0 %copy-start.4 = (bf16[1,1,1,192,2048]{4,3,2,1,0:T(8,128)(2,1)S(1)}, bf16[1,1,1,192,2048]{4,3,2,1,0:T(8,128)(2,1)}, u32[]{:S(2)}) copy-start(bf16[1,1,1,192,2048]{4,3,2,1,0:T(8,128)(2,1)} %param.11) | copy-start | bytes 2359300
  276.1 10.9 %copy-start.5 = (bf16[1,1,1,192,2048]{4,3,2,1,0:T(8,128)(2,1)S(1)}, bf16[1,1,1,192,2048]{4,3,2,1,0:T(8,128)(2,1)}, u32[]{:S(2)}) copy-start(bf16[1,1,1,192,2048]{4,3,2,1,0:T(8,128)(2,1)} %param.12) | copy-start | bytes 2359300
  276.1 14.9 %copy-start.6 = (bf16[1,1,1,192,2048]{4,3,2,1,0:T(8,128)(2,1)S(1)}, bf16[1,1,1,192,2048]{4,3,2,1,0:T(8,128)(2,1)}, u32[]{:S(2)}) copy-start(bf16[1,1,1,192,2048]{4,3,2,1,0:T(8,128)(2,1)} %param.13) | copy-start | bytes 2359300
  283.2 24.2 %collective-permute-start.3 = (bf16[128,1,8,2048]{3,0,2,1:T(8,128)(2,1)}, bf16[128,1,8,2048]{3,0,2,1:T(8,128)(2,1)S(1)}, u32[]{:S(2)}, u32[]{:S(2)}) collective-permute-start(bf16[128,1,8,2048]{3,0,2,1:T(8,128)(2,1)} %reshape.159), channel_id=1, source_target_pairs={{0,1},{1,0},{2,3},{3,2},{4,5},{5,4},{6,7},{7,6},{8,9},{9,8},{10,11... | collective-permute-start | bytes 12582920 | tf_op jit(solution)/shard_map/ppermute | solution.py:12
  285.1 22.2 %collective-permute-start.1 = (bf16[1,192,2048]{2,1,0:T(8,128)(2,1)S(1)}, bf16[1,192,2048]{2,1,0:T(8,128)(2,1)S(1)}, u32[]{:S(2)}, u32[]{:S(2)}) collective-permute-start(bf16[1,192,2048]{2,1,0:T(8,128)(2,1)S(1)} %bitcast.147), channel_id=1, source_target_pairs={{0,2},{1,3},{2,0},{3,1},{4,6},{5,7},{6,4},{7,5},{8,10},{9,11},{10,... | collective-permute-start | bytes 2359304 | tf_op jit(solution)/shard_map/ppermute | solution.py:12
  287.0 37.1 %collective-permute-start.2 = (bf16[1,192,2048]{2,1,0:T(8,128)(2,1)S(1)}, bf16[1,192,2048]{2,1,0:T(8,128)(2,1)S(1)}, u32[]{:S(2)}, u32[]{:S(2)}) collective-permute-start(bf16[1,192,2048]{2,1,0:T(8,128)(2,1)S(1)} %bitcast.150), channel_id=1, source_target_pairs={{0,2},{1,3},{2,0},{3,1},{4,6},{5,7},{6,4},{7,5},{8,10},{9,11},{10,... | collective-permute-start | bytes 2359304 | tf_op jit(solution)/shard_map/ppermute | solution.py:12
  291.0 49.8 %collective-permute-start = (bf16[1,192,2048]{2,1,0:T(8,128)(2,1)S(1)}, bf16[1,192,2048]{2,1,0:T(8,128)(2,1)}, u32[]{:S(2)}, u32[]{:S(2)}) collective-permute-start(bf16[1,192,2048]{2,1,0:T(8,128)(2,1)S(1)} %bitcast.153), channel_id=1, source_target_pairs={{0,2},{1,3},{2,0},{3,1},{4,6},{5,7},{6,4},{7,5},{8,10},{9,11},{10,... | collective-permute-start | bytes 2359304 | tf_op jit(solution)/shard_map/ppermute | solution.py:12
  307.3 3.0 copy-start.7
  307.3 3.0 copy-start.3
  324.2 0.9 copy-start.8
  351.2 24.7 %collective-permute-start.4 = (f32[128,1,8,2048]{3,0,2,1:T(8,128)}, f32[128,1,8,2048]{3,0,2,1:T(8,128)}, u32[]{:S(2)}, u32[]{:S(2)}) collective-permute-start(f32[128,1,8,2048]{3,0,2,1:T(8,128)} %convolution_bitcast_fusion), channel_id=1, source_target_pairs={{0,1},{1,0},{2,3},{3,2},{4,5},{5,4},{6,7},{7,6},{8,9},{9,8},{10,11... | collective-permute-start | bytes 25165832 | tf_op jit(solution)/shard_map/ppermute | solution.py:12
  597.5 7.1 %copy-start.2 = (bf16[64,8]{0,1:T(8,128)(2,1)S(1)}, bf16[64,8]{0,1:T(8,128)(2,1)}, u32[]{:S(2)}) copy-start(bf16[64,8]{0,1:T(8,128)(2,1)} %param.9) | copy-start | bytes 3076
  597.5 68.6 %all-to-all-start.3 = ((bf16[8,16,8,2048]{3,2,0,1:T(8,128)(2,1)}), bf16[8,16,8,2048]{3,2,0,1:T(8,128)(2,1)}, u32[]{:S(2)}, u32[]{:S(2)}) async-start(bf16[8,16,8,2048]{3,2,0,1:T(8,128)(2,1)} %copy.78), calls=%async_computation.3 | async-start | bytes 8388608 | tf_op jit(solution)/shard_map/all_to_all | solution.py:69
  666.2 4.1 copy-start.1
where the time goes:
time: 673 us; the launch traced here: 670 us
  blocking collectives  456 us (68%)
  waiting for transfers between devices  104 us (15%)
  local copies, waits for them, and re-layouts  45.7 us (7%)
  matrix products  32.2 us (5%)
  starting transfers between devices  18.9 us (3%)
  other arithmetic  13 us (2%)
    all_to_all x1, blocking collectives, on_device(): lax.all_to_all(by_rows, 'expert', split_axis=0, concat_axis=0, tiled=True)  206 us
    all_to_all x1, blocking collectives, on_device(): lax.all_to_all(result, 'expert', split_axis=0, concat_axis=0, tiled=True)  194 us
    all_to_all x1, waiting for transfers between devices, on_device(): lax.all_to_all(going_back, 'dp', split_axis=1, concat_axis=1, tiled=True)  60.7 us
    all_to_all x1, blocking collectives, on_device(): lax.all_to_all(outgoing, 'dp', split_axis=1, concat_axis=1, tiled=True)  55.9 us
    ppermute x5, waiting for transfers between devices, swapped(): return lax.ppermute(value, axis, pairs)  43.7 us
    dot_general x2, matrix products, project(): jnp.einsum('bkcf,kfd->bkcd', hidden, down_w, preferred_element_type=jnp.f...  20.9 us
  transfers between devices with their start and end apart: 6, of which 4 were waited for; matrix products, arithmetic and copies ran while one was open for 4% of the time, Pallas kernels for 0%

commit v1 on v0

v1 whole, which is shorter than its diff:
```python
import functools

import jax
import jax.numpy as jnp
from jax import lax
from jax.experimental import pallas as pl
from jax.experimental.pallas import tpu as pltpu
from jax.sharding import PartitionSpec as P

CAP = 8
BF = jnp.bfloat16
F32 = jnp.float32
MESH = pl.DeviceIdType.MESH
RING = 8


def nt(a, b):
    return lax.dot_general(a, b, (((1,), (1,)), ((), ())), preferred_element_type=F32)


def nn(a, b):
    return lax.dot_general(a, b, (((1,), (0,)), ((), ())), preferred_element_type=F32)


def tn(a, b):
    return lax.dot_general(a, b, (((0,), (0,)), ((), ())), preferred_element_type=F32)


def iota(shape, dim):
    return lax.broadcasted_iota(jnp.int32, shape, dim)


def kernel(
    n_rows, ids_ref, wts_ref, place_ref, tok_ref, gate_hbm, up_hbm, down_hbm, out_ref,
    tok, meta_out, meta, disp, arr, yout, ret, stage, rsum, gw, uw, dw, hid,
    tok_send, tok_recv, meta_send, meta_recv, disp_send, arr_recv, y_send, ret_recv,
    rs_send, rs_recv, w_local, w_send, w_cross, w_sib, w_diag,
):
    tokens, width = tok_ref.shape
    half = tokens // 2
    quarter = gate_hbm.shape[3]
    experts = place_ref.shape[1]
    topk = ids_ref.shape[1]
    slots = n_rows * CAP
    row = lax.axis_index("dp")
    col = lax.axis_index("expert")
    g = lax.div(col, 4)
    q = lax.rem(col, 4)

    def ring(step):
        return (row, lax.rem(g + RING + step, RING) * 4 + q)

    sibling = (row, g * 4 + q + 1 - 2 * lax.rem(q, 2))
    cross = (row, g * 4 + lax.rem(q + 2, 4))

    def plane(step):
        return lax.rem(row + step, n_rows)

    def remote(src, dst, send, recv, device):
        return pltpu.make_async_remote_copy(
            src_ref=src, dst_ref=dst, send_sem=send, recv_sem=recv,
            device_id=device, device_id_type=MESH,
        )

    def wait_for(ref, sem):
        pltpu.make_async_copy(ref, ref, sem).wait()

    barrier = pltpu.get_barrier_semaphore()
    partners = [ring(d) for d in range(1, RING)] + [sibling, cross]
    partners += [(plane(j), col) for j in range(1, n_rows)]
    for device in partners:
        pl.semaphore_signal(barrier, inc=1, device_id=device, device_id_type=MESH)

    weights = ((gate_hbm, gw), (up_hbm, uw), (down_hbm, dw))
    for n, (src, dst) in enumerate(weights):
        pltpu.make_async_copy(src.at[0, 0, 0], dst.at[pl.ds(0, quarter)], w_local.at[n]).start()

    lane = iota((tokens, experts), 1)
    hot = jnp.zeros((tokens, experts), F32)
    mix = jnp.zeros((tokens, experts), F32)
    for j in range(topk):
        same = ids_ref[:, j : j + 1] == lane
        hot = hot + jnp.where(same, 1.0, 0.0)
        mix = mix + jnp.where(same, wts_ref[:, j : j + 1], 0.0)
    below = jnp.where(iota((tokens, tokens), 1) < iota((tokens, tokens), 0), 1.0, 0.0).astype(BF)
    earlier = nn(below, hot.astype(BF))
    both = jnp.concatenate([hot * (earlier + 1.0), mix], axis=0).astype(BF)
    order = iota((experts, experts), 0)
    slot_of = lax.rem(order, n_rows) * RING + lax.div(order, n_rows)
    pick = jnp.where(place_ref[...] == slot_of, 1.0, 0.0).astype(BF)
    spread = nt(pick, both)
    meta_out[...] = spread.reshape(RING, n_rows, 2 * tokens)
    tok[0] = tok_ref[...]
    rsum[6, half:] = jnp.zeros((half, width), BF)
    rsum[7, :half] = jnp.zeros((half, width), BF)

    pl.semaphore_wait(barrier, len(partners))

    own_up = remote(tok.at[0], tok.at[1], tok_send.at[0], tok_recv.at[1], ring(1))
    own_down = remote(tok.at[0], tok.at[2], tok_send.at[7], tok_recv.at[2], ring(-1))
    meta_copies = []
    for slot, step in ((1, 1), (2, -1), (3, 2), (4, -2), (5, 3), (6, -3), (7, 4)):
        there = lax.rem(g + RING + step, RING)
        meta_copies.append(
            remote(meta_out.at[there], meta.at[slot], meta_send.at[slot], meta_recv.at[slot], ring(step))
        )
    for copy in meta_copies:
        copy.start()
    own_up.start()
    own_down.start()
    meta[0] = meta_out[g]
    cross_copies = [
        remote(src.at[0, 0, 0], dst.at[pl.ds(2 * quarter, quarter)], w_send.at[n], w_cross.at[n], cross)
        for n, (src, dst) in enumerate(weights)
    ]
    sib_copies = [
        remote(src.at[0, 0, 0], dst.at[pl.ds(quarter, quarter)], w_send.at[3 + n], w_sib.at[n], sibling)
        for n, (src, dst) in enumerate(weights)
    ]
    diag_copies = [
        remote(dst.at[pl.ds(2 * quarter, quarter)], dst.at[pl.ds(3 * quarter, quarter)], w_send.at[6 + n], w_diag.at[n], sibling)
        for n, (_, dst) in enumerate(weights)
    ]
    for copy in cross_copies + sib_copies:
        copy.start()

    grow = jnp.where(lax.div(iota((slots, n_rows), 0), CAP) == iota((slots, n_rows), 1), 1.0, 0.0)
    place_in = (lax.rem(iota((slots, tokens), 0), CAP) + 1).astype(F32)

    def send_rows(i, src, dst, send, recv):
        pltpu.make_async_copy(src.at[i, row], dst.at[i, row], recv.at[i]).start()
        for j in range(1, n_rows):
            there = plane(j)
            remote(src.at[i, there], dst.at[i, row], send.at[i], recv.at[i], (there, col)).start()

    wide = min(512, width)

    def dispatch(i, _):
        @pl.when(i > 0)
        def _():
            wait_for(tok.at[i], tok_recv.at[i])
            wait_for(meta.at[i], meta_recv.at[i])

        @pl.when((i >= 1) & (i <= 4))
        def _():
            remote(tok.at[i], tok.at[i + 2], tok_send.at[i], tok_recv.at[i + 2], ring(2 * lax.rem(i, 2) - 1)).start()

        @pl.when(i == 5)
        def _():
            remote(tok.at[5, pl.ds(0, half)], tok.at[7, pl.ds(0, half)], tok_send.at[5], tok_recv.at[7], ring(1)).start()

        @pl.when(i == 6)
        def _():
            remote(tok.at[6, pl.ds(half, half)], tok.at[7, pl.ds(half, half)], tok_send.at[6], tok_recv.at[7], ring(-1)).start()

        grown = nn(grow, meta[i])
        hot_rows = jnp.where(grown[:, :tokens] == place_in, 1.0, 0.0).astype(BF)
        for n in range(0, width, wide):
            rows = nn(hot_rows, tok[i, :, n : n + wide])
            disp[i, :, :, n : n + wide] = rows.reshape(n_rows, CAP, wide).astype(BF)
        send_rows(i, disp, arr, disp_send, arr_recv)
        return 0

    lax.fori_loop(0, RING, dispatch, 0)

    for n, (src, dst) in enumerate(weights):
        cross_copies[n].wait_recv()
        diag_copies[n].start()
    for n, (src, dst) in enumerate(weights):
        pltpu.make_async_copy(src.at[0, 0, 0], dst.at[pl.ds(0, quarter)], w_local.at[n]).wait()
        sib_copies[n].wait_recv()
        diag_copies[n].wait_recv()

    hidden = gw.shape[0]
    tile = hidden // 3

    def expert(k, _):
        i = RING - 1 - k
        wait_for(arr.at[i], arr_recv.at[i])
        x = arr[i].astype(F32).reshape(slots, width).astype(BF)
        for h in range(0, hidden, tile):
            gate = nt(x, gw[h : h + tile, :])
            up = nt(x, uw[h : h + tile, :])
            hid[:, h : h + tile] = (gate / (1.0 + jnp.exp(-gate)) * up).astype(BF)
        for n in range(0, width, wide):
            y = nn(hid[...], dw[:, n : n + wide])
            yout[i, :, :, n : n + wide] = y.reshape(n_rows, CAP, wide).astype(BF)
        send_rows(i, yout, ret, y_send, ret_recv)
        return 0

    lax.fori_loop(0, RING, expert, 0)

    def mixing(i):
        wait_for(ret.at[i], ret_recv.at[i])
        grown = nn(grow, meta[i])
        return jnp.where(grown[:, :tokens] == place_in, grown[:, tokens:], 0.0).astype(BF)

    def part(i, mixer, n):
        rows = ret[i, :, :, n : n + wide].astype(F32).reshape(slots, wide).astype(BF)
        return tn(mixer, rows)

    mixer = mixing(7)
    for n in range(0, width, wide):
        stage[7, :, n : n + wide] = part(7, mixer, n).astype(BF)
    far = (
        remote(stage.at[7, pl.ds(0, half)], rsum.at[6, pl.ds(0, half)], rs_send.at[7], rs_recv.at[6], ring(-1)),
        remote(stage.at[7, pl.ds(half, half)], rsum.at[7, pl.ds(half, half)], rs_send.at[0], rs_recv.at[7], ring(1)),
    )
    for copy in far:
        copy.start()

    def reduce(k, _):
        i = 6 - k
        mixer = mixing(i)

        @pl.when(i >= 5)
        def _():
            wait_for(rsum.at[i + 1, pl.ds(0, half)], rs_recv.at[i + 1])

        @pl.when(i <= 4)
        def _():
            wait_for(rsum.at[i + 1], rs_recv.at[i + 1])

        for n in range(0, width, wide):
            total = part(i, mixer, n) + rsum[i + 1, :, n : n + wide].astype(F32)
            stage[i, :, n : n + wide] = total.astype(BF)
        remote(stage.at[i], rsum.at[i - 1], rs_send.at[i], rs_recv.at[i - 1], ring(1 - 2 * lax.rem(i, 2))).start()
        return 0

    lax.fori_loop(0, 6, reduce, 0)

    mixer = mixing(0)
    wait_for(rsum.at[0], rs_recv.at[0])
    wait_for(rsum.at[1], rs_recv.at[1])
    for n in range(0, width, wide):
        near = rsum[0, :, n : n + wide].astype(F32) + rsum[1, :, n : n + wide].astype(F32)
        out_ref[:, n : n + wide] = (part(0, mixer, n) + near).astype(BF)

    own_up.wait_send()
    own_down.wait_send()
    for copy in meta_copies + cross_copies + sib_copies + diag_copies:
        copy.wait_send()
    for copy in far:
        copy.wait_send()

    def drain(i, _):
        wait_for(disp.at[i, pl.ds(0, n_rows - 1)], disp_send.at[i])
        wait_for(yout.at[i, pl.ds(0, n_rows - 1)], y_send.at[i])

        @pl.when((i >= 1) & (i <= 4))
        def _():
            wait_for(tok.at[i], tok_send.at[i])

        @pl.when((i == 5) | (i == 6))
        def _():
            wait_for(tok.at[i, pl.ds(0, half)], tok_send.at[i])

        @pl.when((i >= 1) & (i <= 6))
        def _():
            wait_for(stage.at[i], rs_send.at[i])

        return 0

    lax.fori_loop(0, RING, drain, 0)


def on_device(n_rows, tokens, route_ids, route_weights, placement, gate_proj, up_proj, down_proj):
    count, width = tokens.shape
    quarter = gate_proj.shape[3]
    experts = placement.shape[0]
    blocks = (RING, n_rows, CAP, width)
    vmem = pl.BlockSpec(memory_space=pltpu.VMEM)
    hbm = pl.BlockSpec(memory_space=pl.ANY)
    dma = pltpu.SemaphoreType.DMA
    scratch = [
        pltpu.VMEM((RING, count, width), BF),
        pltpu.VMEM((RING, n_rows, 2 * count), F32),
        pltpu.VMEM((RING, n_rows, 2 * count), F32),
        pltpu.VMEM(blocks, BF),
        pltpu.VMEM(blocks, BF),
        pltpu.VMEM(blocks, BF),
        pltpu.VMEM(blocks, BF),
        pltpu.VMEM((RING, count, width), BF),
        pltpu.VMEM((RING, count, width), BF),
        pltpu.VMEM((4 * quarter, width), BF),
        pltpu.VMEM((4 * quarter, width), BF),
        pltpu.VMEM((4 * quarter, width), BF),
        pltpu.VMEM((n_rows * CAP, 4 * quarter), BF),
    ]
    scratch += [dma((RING,)) for _ in range(10)]
    scratch += [dma((3,)), dma((9,)), dma((3,)), dma((3,)), dma((3,))]
    return pl.pallas_call(
        functools.partial(kernel, n_rows),
        out_shape=jax.ShapeDtypeStruct((count, width), BF),
        in_specs=[vmem, vmem, vmem, vmem, hbm, hbm, hbm],
        out_specs=vmem,
        scratch_shapes=scratch,
        compiler_params=pltpu.CompilerParams(
            collective_id=0, has_side_effects=True, vmem_limit_bytes=60 * 2**20
        ),
    )(
        route_ids,
        route_weights.astype(F32),
        placement.reshape(1, experts),
        tokens,
        gate_proj,
        up_proj,
        down_proj,
    )


def solution(mesh):
    in_specs = (
        P(("dp", "expert"), None),
        P(("dp", "expert"), None),
        P(("dp", "expert"), None),
        P(),
        P("dp", "expert", None, None, None),
        P("dp", "expert", None, None, None),
        P("dp", "expert", None, None, None),
    )
    return jax.shard_map(
        functools.partial(on_device, mesh.shape["dp"]),
        mesh=mesh,
        in_specs=in_specs,
        out_specs=P(("dp", "expert"), None),
        check_vma=False,
    )
```

time: 673 us -> 199 us (0.30)
  blocking collectives: 456 us -> 0 us
  Pallas kernels: 0 us -> 195 us
  waiting for transfers between devices: 104 us -> 0 us
  local copies, waits for them, and re-layouts: 45.7 us -> 3.76 us
  matrix products: 32.2 us -> 0 us
  starting transfers between devices: 18.9 us -> 0 us
  other arithmetic: 13 us -> 0 us
    all_to_all x3 -> x0, blocking collectives: 456 us -> none  [the longest x1 206 us: on_device(): lax.all_to_all(by_rows, 'expert', split_axis=0, concat_axis=0, tiled=True)]
    pallas_call x0 -> x1, Pallas kernels: none -> 195 us  [on_device(): pl.pallas_call(functools.partial(kernel, n_rows), out_shape=jax.ShapeDtyp...]
    all_to_all x1 -> x0, waiting for transfers between devices: 60.7 us -> none  [on_device(): lax.all_to_all(going_back, 'dp', split_axis=1, concat_axis=1, tiled=True)]
    ppermute x5 -> x0, waiting for transfers between devices: 43.7 us -> none  [swapped(): return lax.ppermute(value, axis, pairs)]
    dot_general x6 -> x0, matrix products: 32.2 us -> none  [the longest x2 20.9 us: project(): jnp.einsum('bkcf,kfd->bkcd', hidden, down_w, preferred_element_type=jnp.f...]
    reshape x7 -> x0, local copies, waits for them, and re-layouts: 25.4 us -> none  [the longest x2 11.4 us: on_device(): result = result.reshape(n_cols, subsets * per_slot, capacity, width)]
    ppermute x5 -> x0, starting transfers between devices: 11.8 us -> none  [swapped(): return lax.ppermute(value, axis, pairs)]
    all_to_all x4 -> x0, local copies, waits for them, and re-layouts: 11.2 us -> none  [the longest x1 4.39 us: on_device(): lax.all_to_all(result, 'expert', split_axis=0, concat_axis=0, tiled=True)]
  transfers between devices with their start and end apart: 6 -> 0, of which waited for: 4 -> 0; matrix products, arithmetic and copies ran while one was open for 4% -> 0% of each run, Pallas kernels for 0% -> 0%
where the time goes in v1:
time: 199 us
  Pallas kernels  195 us (98%)
  local copies, waits for them, and re-layouts  3.76 us (2%)
    pallas_call x1, Pallas kernels, on_device(): pl.pallas_call(functools.partial(kernel, n_rows), out_shape=jax.ShapeDtyp...  195 us

profile of v1, /device:TPU:6, one launch (start us, length us, event | category | flops | bytes accessed | tf_op | source)
XLA Modules:
  0.0 199.1 jit_solution(17037481717990517545)
XLA Ops:
  0.0 0.0 copy-start
  0.0 1.4 copy.10.ids_ref
  1.4 0.0 copy-done
  1.4 0.7 copy.11.wts_ref
  2.1 195.3 %shard_map.73 = bf16[64,2048]{1,0:T(8,128)(2,1)} custom-call(s32[64,8]{1,0:T(8,128)} %copy.10.ids_ref, f32[64,8]{1,0:T(8,128)} %copy.11.wts_ref, s32[1,128]{1,0:T(1,128)} %bitcast.1, bf16[64,2048]{1,0:T(8,128)(2,1)} %tok_ref.1, bf16[1,1,1,192,2048]{4,3,2,1,0:T(8,128)(2,1)} %gate_hbm.1, bf16[1,1,1,192,2048]{4,3,2,1,0:T(8,128)(2,1)} %up_hbm.1, ...), custom_call_target="tpu_custom_call" | custom-call | tf_op jit(solution)/shard_map/pallas_call | solution.py:292
  197.4 1.7 copy.13
Async XLA Ops:
  0.0 1.4 copy-start

commit v2 on v1

v2 whole, which is shorter than its diff:
```python
import functools

import jax
import jax.numpy as jnp
from jax import lax
from jax.experimental import pallas as pl
from jax.experimental.pallas import tpu as pltpu
from jax.sharding import PartitionSpec as P

CAP = 8
BF = jnp.bfloat16
F32 = jnp.float32
MESH = pl.DeviceIdType.MESH
RING = 8


def nt(a, b):
    return lax.dot_general(a, b, (((1,), (1,)), ((), ())), preferred_element_type=F32)


def nn(a, b):
    return lax.dot_general(a, b, (((1,), (0,)), ((), ())), preferred_element_type=F32)


def tn(a, b):
    return lax.dot_general(a, b, (((0,), (0,)), ((), ())), preferred_element_type=F32)


def iota(shape, dim):
    return lax.broadcasted_iota(jnp.int32, shape, dim)


def kernel(
    n_rows, ids_ref, wts_ref, place_ref, tok_ref, gate_hbm, up_hbm, down_hbm, out_ref,
    tok, meta_out, meta, disp, arr, yout, ret, stage, rsum, gw, uw, dw, hid,
    tok_send, tok_recv, meta_send, meta_recv, disp_send, arr_recv, y_send, ret_recv,
    rs_send, rs_recv, w_local, w_send, w_cross, w_sib, w_diag,
):
    tokens, width = tok_ref.shape
    quarter = gate_hbm.shape[3]
    experts = place_ref.shape[1]
    topk = ids_ref.shape[0]
    slots = n_rows * CAP
    row = lax.axis_index("dp")
    col = lax.axis_index("expert")
    g = lax.div(col, 4)
    q = lax.rem(col, 4)

    way = 1 - 2 * lax.div(q, 2)
    facing = lax.rem(q + 2, 4)

    def ring(step, part):
        return (row, lax.rem(g + RING + way * step, RING) * 4 + part)

    down = ring(1, q)
    up = ring(-1, q)
    across = ring(-1, facing)
    readers = [(d, part) for d in (1, 2, 3) for part in (0, 1)] + [(4, 0)]

    def reader(d, part):
        return ring(-d, facing) if part else ring(d, q)

    sibling = (row, g * 4 + q + 1 - 2 * lax.rem(q, 2))
    cross = (row, g * 4 + facing)

    def plane(step):
        return lax.rem(row + step, n_rows)

    def remote(src, dst, send, recv, device):
        return pltpu.make_async_remote_copy(
            src_ref=src, dst_ref=dst, send_sem=send, recv_sem=recv,
            device_id=device, device_id_type=MESH,
        )

    def wait_for(ref, sem):
        pltpu.make_async_copy(ref, ref, sem).wait()

    barrier = pltpu.get_barrier_semaphore()
    partners = [reader(d, part) for d, part in readers]
    partners += [ring(-d, q) for d in (1, 2, 3)]
    partners += [sibling, cross]
    partners += [(plane(j), col) for j in range(1, n_rows)]
    for device in partners:
        pl.semaphore_signal(barrier, inc=1, device_id=device, device_id_type=MESH)

    weights = ((gate_hbm, gw), (up_hbm, uw), (down_hbm, dw))
    for n, (src, dst) in enumerate(weights):
        pltpu.make_async_copy(src.at[0, 0, 0], dst.at[pl.ds(0, quarter)], w_local.at[n]).start()

    name = iota((experts, tokens), 0)
    hot = jnp.zeros((experts, tokens), F32)
    mix = jnp.zeros((experts, tokens), F32)
    for j in range(topk):
        same = ids_ref[j : j + 1, :] == name
        hot = hot + jnp.where(same, 1.0, 0.0)
        mix = mix + jnp.where(same, wts_ref[j : j + 1, :].astype(F32), 0.0)
    before = jnp.where(iota((tokens, tokens), 0) < iota((tokens, tokens), 1), 1.0, 0.0).astype(BF)
    earlier = nn(hot.astype(BF), before)
    order = iota((experts, experts), 0)
    slot_of = lax.rem(order, n_rows) * RING + lax.div(order, n_rows)
    pick = jnp.where(place_ref[...] == slot_of, 1.0, 0.0).astype(BF)
    place_to = nn(pick, (hot * (earlier + 1.0)).astype(BF))
    meta_out[:, :, :tokens] = place_to.reshape(RING, n_rows, tokens)
    meta_out[:, :, tokens:] = nn(pick, mix.astype(BF)).reshape(RING, n_rows, tokens)
    tok[0] = tok_ref[...]

    pl.semaphore_wait(barrier, len(partners))

    own_copies = [
        remote(tok.at[0], tok.at[1], tok_send.at[0], tok_recv.at[1], down),
        remote(tok.at[0], tok.at[2], tok_send.at[7], tok_recv.at[2], across),
    ]
    meta_copies = []
    for slot, (d, part) in enumerate(readers, 1):
        there = lax.rem(g + RING + way * (-d if part else d), RING)
        meta_copies.append(
            remote(meta_out.at[there], meta.at[slot], meta_send.at[slot], meta_recv.at[slot], reader(d, part))
        )
    for copy in meta_copies + own_copies:
        copy.start()
    meta[0] = meta_out[g]
    piece = quarter // 2

    def moved(dst, source, n, to):
        return dst.at[pl.ds(to * quarter + n * piece, piece)] if source is None else source.at[0, 0, 0, pl.ds(n * piece, piece)]

    cross_copies, sib_copies, diag_copies = [], [], []
    for w, (src, dst) in enumerate(weights):
        for n in range(2):
            k = 2 * w + n
            mine = moved(dst, src, n, 0)
            cross_copies.append(remote(mine, moved(dst, None, n, 2), w_send.at[k], w_cross.at[k], cross))
            sib_copies.append(remote(mine, moved(dst, None, n, 1), w_send.at[6 + k], w_sib.at[k], sibling))
            diag_copies.append(
                remote(moved(dst, None, n, 2), moved(dst, None, n, 3), w_send.at[12 + k], w_diag.at[k], sibling)
            )

    grow = jnp.where(lax.div(iota((slots, n_rows), 0), CAP) == iota((slots, n_rows), 1), 1.0, 0.0)
    place_in = (lax.rem(iota((slots, tokens), 0), CAP) + 1).astype(F32)

    def send_rows(i, src, dst, send, recv):
        pltpu.make_async_copy(src.at[i, row], dst.at[i, row], recv.at[i]).start()
        for j in range(1, n_rows):
            there = plane(j)
            remote(src.at[i, there], dst.at[i, row], send.at[i], recv.at[i], (there, col)).start()

    wide = min(512, width)

    def dispatch(i, _):
        @pl.when(i > 0)
        def _():
            wait_for(tok.at[i], tok_recv.at[i])
            wait_for(meta.at[i], meta_recv.at[i])

        @pl.when((i >= 1) & (i <= 5))
        def _():
            remote(tok.at[i], tok.at[i + 2], tok_send.at[i], tok_recv.at[i + 2], down).start()

        @pl.when(i == 5)
        def _():
            for copy in cross_copies + sib_copies:
                copy.start()

        grown = nn(grow, meta[i])
        hot_rows = jnp.where(grown[:, :tokens] == place_in, 1.0, 0.0).astype(BF)
        for n in range(0, width, wide):
            rows = nn(hot_rows, tok[i, :, n : n + wide])
            disp[i, :, :, n : n + wide] = rows.reshape(n_rows, CAP, wide).astype(BF)
        send_rows(i, disp, arr, disp_send, arr_recv)
        return 0

    lax.fori_loop(0, RING, dispatch, 0)

    def take(n):
        for k in range(2 * n, 2 * n + 2):
            cross_copies[k].wait_recv()
            diag_copies[k].start()

    def have(n):
        src, dst = weights[n]
        pltpu.make_async_copy(src.at[0, 0, 0], dst.at[pl.ds(0, quarter)], w_local.at[n]).wait()
        for k in range(2 * n, 2 * n + 2):
            sib_copies[k].wait_recv()
            diag_copies[k].wait_recv()

    hidden = gw.shape[0]
    tile = hidden // 3

    def gated(k, _):
        wait_for(arr.at[2 * k], arr_recv.at[2 * k])
        wait_for(arr.at[2 * k + 1], arr_recv.at[2 * k + 1])
        x = arr[pl.ds(2 * k, 2)].astype(F32).reshape(2 * slots, width).astype(BF)
        for h in range(0, hidden, tile):
            gate = nt(x, gw[h : h + tile, :])
            up = nt(x, uw[h : h + tile, :])
            kept = (gate / (1.0 + jnp.exp(-gate)) * up).astype(BF)
            hid[pl.ds(2 * k, 2), :, h : h + tile] = kept.reshape(2, slots, tile)
        return 0

    def projected(k, _):
        i = RING - 1 - k
        for n in range(0, width, wide):
            y = nn(hid[i], dw[:, n : n + wide])
            yout[i, :, :, n : n + wide] = y.reshape(n_rows, CAP, wide).astype(BF)
        send_rows(i, yout, ret, y_send, ret_recv)
        return 0

    take(0)
    take(1)
    have(0)
    have(1)
    lax.fori_loop(0, RING // 2, gated, 0)
    take(2)
    have(2)
    lax.fori_loop(0, RING, projected, 0)

    def mixing(i):
        wait_for(ret.at[i], ret_recv.at[i])
        grown = nn(grow, meta[i])
        return jnp.where(grown[:, :tokens] == place_in, grown[:, tokens:], 0.0).astype(BF)

    def part(i, mixer, n):
        rows = ret[i, :, :, n : n + wide].astype(F32).reshape(slots, wide).astype(BF)
        return tn(mixer, rows)

    def reduce(k, _):
        i = RING - 1 - k
        mixer = mixing(i)

        @pl.when(i <= 5)
        def _():
            wait_for(rsum.at[i + 1], rs_recv.at[i + 1])
            for n in range(0, width, wide):
                total = part(i, mixer, n) + rsum[i + 1, :, n : n + wide].astype(F32)
                stage[i, :, n : n + wide] = total.astype(BF)

        @pl.when(i > 5)
        def _():
            for n in range(0, width, wide):
                stage[i, :, n : n + wide] = part(i, mixer, n).astype(BF)

        @pl.when(i != 2)
        def _():
            remote(stage.at[i], rsum.at[i - 1], rs_send.at[i], rs_recv.at[i - 1], up).start()

        @pl.when(i == 2)
        def _():
            remote(stage.at[2], rsum.at[1], rs_send.at[2], rs_recv.at[1], across).start()

        return 0

    lax.fori_loop(0, RING - 1, reduce, 0)

    mixer = mixing(0)
    wait_for(rsum.at[0], rs_recv.at[0])
    wait_for(rsum.at[1], rs_recv.at[1])
    for n in range(0, width, wide):
        near = rsum[0, :, n : n + wide].astype(F32) + rsum[1, :, n : n + wide].astype(F32)
        out_ref[:, n : n + wide] = (part(0, mixer, n) + near).astype(BF)

    for copy in own_copies + meta_copies + cross_copies + sib_copies + diag_copies:
        copy.wait_send()

    def drain(i, _):
        wait_for(disp.at[i, pl.ds(0, n_rows - 1)], disp_send.at[i])
        wait_for(yout.at[i, pl.ds(0, n_rows - 1)], y_send.at[i])

        @pl.when((i >= 1) & (i <= 5))
        def _():
            wait_for(tok.at[i], tok_send.at[i])

        @pl.when(i >= 1)
        def _():
            wait_for(stage.at[i], rs_send.at[i])

        return 0

    lax.fori_loop(0, RING, drain, 0)


def on_device(n_rows, tokens, route_ids, route_weights, placement, gate_proj, up_proj, down_proj):
    count, width = tokens.shape
    quarter = gate_proj.shape[3]
    experts = placement.shape[0]
    blocks = (RING, n_rows, CAP, width)
    vmem = pl.BlockSpec(memory_space=pltpu.VMEM)
    hbm = pl.BlockSpec(memory_space=pl.ANY)
    dma = pltpu.SemaphoreType.DMA
    scratch = [
        pltpu.VMEM((RING, count, width), BF),
        pltpu.VMEM((RING, n_rows, 2 * count), F32),
        pltpu.VMEM((RING, n_rows, 2 * count), F32),
        pltpu.VMEM(blocks, BF),
        pltpu.VMEM(blocks, BF),
        pltpu.VMEM(blocks, BF),
        pltpu.VMEM(blocks, BF),
        pltpu.VMEM((RING, count, width), BF),
        pltpu.VMEM((RING, count, width), BF),
        pltpu.VMEM((4 * quarter, width), BF),
        pltpu.VMEM((4 * quarter, width), BF),
        pltpu.VMEM((4 * quarter, width), BF),
        pltpu.VMEM((RING, n_rows * CAP, 4 * quarter), BF),
    ]
    scratch += [dma((RING,)) for _ in range(10)]
    scratch += [dma((3,)), dma((18,)), dma((6,)), dma((6,)), dma((6,))]
    return pl.pallas_call(
        functools.partial(kernel, n_rows),
        out_shape=jax.ShapeDtypeStruct((count, width), BF),
        in_specs=[vmem, vmem, vmem, vmem, hbm, hbm, hbm],
        out_specs=vmem,
        scratch_shapes=scratch,
        compiler_params=pltpu.CompilerParams(
            collective_id=0, has_side_effects=True, vmem_limit_bytes=60 * 2**20
        ),
    )(
        route_ids.T,
        route_weights.T,
        placement.reshape(1, experts),
        tokens,
        gate_proj,
        up_proj,
        down_proj,
    )


def solution(mesh):
    in_specs = (
        P(("dp", "expert"), None),
        P(("dp", "expert"), None),
        P(("dp", "expert"), None),
        P(),
        P("dp", "expert", None, None, None),
        P("dp", "expert", None, None, None),
        P("dp", "expert", None, None, None),
    )
    return jax.shard_map(
        functools.partial(on_device, mesh.shape["dp"]),
        mesh=mesh,
        in_specs=in_specs,
        out_specs=P(("dp", "expert"), None),
        check_vma=False,
    )
```

time: 199 us -> 173 us (0.87)
  the two profiles are of different devices: /device:TPU:6 before, /device:TPU:181 now
where the time goes in v2:
time: 173 us
  Pallas kernels  171 us (99%)
    pallas_call x1, Pallas kernels, on_device(): pl.pallas_call(functools.partial(kernel, n_rows), out_shape=jax.ShapeDtyp...  171 us

profile of v2, /device:TPU:181, one launch (start us, length us, event | category | flops | bytes accessed | tf_op | source)
XLA Modules:
  0.0 173.0 jit_solution(12140303845974812194)
XLA Ops:
  0.0 171.3 %shard_map.73 = bf16[64,2048]{1,0:T(8,128)(2,1)} custom-call(s32[8,64]{1,0:T(8,128)} %bitcast.3, bf16[8,64]{1,0:T(8,128)(2,1)} %bitcast.4, s32[1,128]{1,0:T(1,128)} %bitcast.5, bf16[64,2048]{1,0:T(8,128)(2,1)} %tok_ref.1, bf16[1,1,1,192,2048]{4,3,2,1,0:T(8,128)(2,1)} %gate_hbm.1, bf16[1,1,1,192,2048]{4,3,2,1,0:T(8,128)(2,1)} %up_hbm.1, ...), custom_call_target="tpu_custom_call" | custom-call | tf_op jit(solution)/shard_map/pallas_call | solution.py:306
  171.3 1.7 copy.9

commit v3 on v2

--- a/solution.py
+++ b/solution.py
@@ -83,9 +83,22 @@
     for device in partners:
         pl.semaphore_signal(barrier, inc=1, device_id=device, device_id_type=MESH)
 
-    weights = ((gate_hbm, gw), (up_hbm, uw), (down_hbm, dw))
-    for n, (src, dst) in enumerate(weights):
-        pltpu.make_async_copy(src.at[0, 0, 0], dst.at[pl.ds(0, quarter)], w_local.at[n]).start()
+    piece = quarter // 2
+    side = width // 2
+
+    def given(k):
+        if k < 4:
+            return (gate_hbm, up_hbm)[k // 2].at[0, 0, 0, pl.ds(k % 2 * piece, piece)]
+        return down_hbm.at[0, 0, 0, :, pl.ds((k - 4) * side, side)]
+
+    def kept(k, place):
+        if k < 4:
+            return (gw, uw)[k // 2].at[pl.ds(place * quarter + k % 2 * piece, piece)]
+        return dw.at[k - 4, pl.ds(place * quarter, quarter)]
+
+    local_copies = [pltpu.make_async_copy(given(k), kept(k, 0), w_local.at[k]) for k in range(6)]
+    for copy in local_copies:
+        copy.start()
 
     name = iota((experts, tokens), 0)
     hot = jnp.zeros((experts, tokens), F32)
@@ -119,32 +132,21 @@
     for copy in meta_copies + own_copies:
         copy.start()
     meta[0] = meta_out[g]
-    piece = quarter // 2
-
-    def moved(dst, source, n, to):
-        return dst.at[pl.ds(to * quarter + n * piece, piece)] if source is None else source.at[0, 0, 0, pl.ds(n * piece, piece)]
-
-    cross_copies, sib_copies, diag_copies = [], [], []
-    for w, (src, dst) in enumerate(weights):
-        for n in range(2):
-            k = 2 * w + n
-            mine = moved(dst, src, n, 0)
-            cross_copies.append(remote(mine, moved(dst, None, n, 2), w_send.at[k], w_cross.at[k], cross))
-            sib_copies.append(remote(mine, moved(dst, None, n, 1), w_send.at[6 + k], w_sib.at[k], sibling))
-            diag_copies.append(
-                remote(moved(dst, None, n, 2), moved(dst, None, n, 3), w_send.at[12 + k], w_diag.at[k], sibling)
-            )
+    cross_copies = [remote(given(k), kept(k, 2), w_send.at[k], w_cross.at[k], cross) for k in range(6)]
+    sib_copies = [remote(given(k), kept(k, 1), w_send.at[6 + k], w_sib.at[k], sibling) for k in range(6)]
+    diag_copies = [remote(kept(k, 2), kept(k, 3), w_send.at[12 + k], w_diag.at[k], sibling) for k in range(6)]
+    cross_copies[0].start()
 
     grow = jnp.where(lax.div(iota((slots, n_rows), 0), CAP) == iota((slots, n_rows), 1), 1.0, 0.0)
     place_in = (lax.rem(iota((slots, tokens), 0), CAP) + 1).astype(F32)
 
-    def send_rows(i, src, dst, send, recv):
-        pltpu.make_async_copy(src.at[i, row], dst.at[i, row], recv.at[i]).start()
+    def send_rows(src, dst, send, recv):
+        pltpu.make_async_copy(src.at[row], dst.at[row], recv).start()
         for j in range(1, n_rows):
             there = plane(j)
-            remote(src.at[i, there], dst.at[i, row], send.at[i], recv.at[i], (there, col)).start()
-
-    wide = min(512, width)
+            remote(src.at[there], dst.at[row], send, recv, (there, col)).start()
+
+    wide = min(512, side)
 
     def dispatch(i, _):
         @pl.when(i > 0)
@@ -156,9 +158,13 @@
         def _():
             remote(tok.at[i], tok.at[i + 2], tok_send.at[i], tok_recv.at[i + 2], down).start()
 
+        @pl.when(i == 2)
+        def _():
+            cross_copies[1].start()
+
         @pl.when(i == 5)
         def _():
-            for copy in cross_copies + sib_copies:
+            for copy in cross_copies[2:] + sib_copies:
                 copy.start()
 
         grown = nn(grow, meta[i])
@@ -166,20 +172,19 @@
         for n in range(0, width, wide):
             rows = nn(hot_rows, tok[i, :, n : n + wide])
             disp[i, :, :, n : n + wide] = rows.reshape(n_rows, CAP, wide).astype(BF)
-        send_rows(i, disp, arr, disp_send, arr_recv)
+        send_rows(disp.at[i], arr.at[i], disp_send.at[i], arr_recv.at[i])
         return 0
 
     lax.fori_loop(0, RING, dispatch, 0)
 
-    def take(n):
-        for k in range(2 * n, 2 * n + 2):
+    def take(*pieces):
+        for k in pieces:
             cross_copies[k].wait_recv()
             diag_copies[k].start()
 
-    def have(n):
-        src, dst = weights[n]
-        pltpu.make_async_copy(src.at[0, 0, 0], dst.at[pl.ds(0, quarter)], w_local.at[n]).wait()
-        for k in range(2 * n, 2 * n + 2):
+    def have(*pieces):
+        for k in pieces:
+            local_copies[k].wait()
             sib_copies[k].wait_recv()
             diag_copies[k].wait_recv()
 
@@ -193,77 +198,90 @@
         for h in range(0, hidden, tile):
             gate = nt(x, gw[h : h + tile, :])
             up = nt(x, uw[h : h + tile, :])
-            kept = (gate / (1.0 + jnp.exp(-gate)) * up).astype(BF)
-            hid[pl.ds(2 * k, 2), :, h : h + tile] = kept.reshape(2, slots, tile)
+            both = (gate / (1.0 + jnp.exp(-gate)) * up).astype(BF)
+            hid[pl.ds(2 * k, 2), :, h : h + tile] = both.reshape(2, slots, tile)
         return 0
 
-    def projected(k, _):
-        i = RING - 1 - k
-        for n in range(0, width, wide):
-            y = nn(hid[i], dw[:, n : n + wide])
-            yout[i, :, :, n : n + wide] = y.reshape(n_rows, CAP, wide).astype(BF)
-        send_rows(i, yout, ret, y_send, ret_recv)
+    take(0, 1, 2, 3)
+    have(0, 1, 2, 3)
+    lax.fori_loop(0, RING // 2, gated, 0)
+    take(4)
+    have(4)
+
+    def projected(h, i):
+        for n in range(0, side, wide):
+            y = nn(hid[i], dw[h, :, n : n + wide])
+            yout[h, i, :, :, n : n + wide] = y.reshape(n_rows, CAP, wide).astype(BF)
+        send_rows(yout.at[h, i], ret.at[h, i], y_send.at[h, i], ret_recv.at[h, i])
+
+    def part(h, i, mixer, n):
+        rows = ret[h, i, :, :, n : n + wide].astype(F32).reshape(slots, wide).astype(BF)
+        return tn(mixer, rows)
+
+    def summed(h, i):
+        wait_for(ret.at[h, i], ret_recv.at[h, i])
+        grown = nn(grow, meta[i])
+        mixer = jnp.where(grown[:, :tokens] == place_in, grown[:, tokens:], 0.0).astype(BF)
+
+        @pl.when((i >= 1) & (i <= 5))
+        def _():
+            wait_for(rsum.at[h, i + 1], rs_recv.at[h, i + 1])
+            for n in range(0, side, wide):
+                total = part(h, i, mixer, n) + rsum[h, i + 1, :, n : n + wide].astype(F32)
+                stage[h, i, :, n : n + wide] = total.astype(BF)
+
+        @pl.when(i > 5)
+        def _():
+            for n in range(0, side, wide):
+                stage[h, i, :, n : n + wide] = part(h, i, mixer, n).astype(BF)
+
+        @pl.when((i >= 1) & (i != 2))
+        def _():
+            remote(stage.at[h, i], rsum.at[h, i - 1], rs_send.at[h, i], rs_recv.at[h, i - 1], up).start()
+
+        @pl.when(i == 2)
+        def _():
+            remote(stage.at[h, 2], rsum.at[h, 1], rs_send.at[h, 2], rs_recv.at[h, 1], across).start()
+
+        @pl.when(i == 0)
+        def _():
+            wait_for(rsum.at[h, 0], rs_recv.at[h, 0])
+            wait_for(rsum.at[h, 1], rs_recv.at[h, 1])
+            for n in range(0, side, wide):
+                near = rsum[h, 0, :, n : n + wide].astype(F32) + rsum[h, 1, :, n : n + wide].astype(F32)
+                at = pl.multiple_of(h * side + n, wide)
+                out_ref[:, pl.ds(at, wide)] = (part(h, 0, mixer, n) + near).astype(BF)
+
+    lag = 3
+
+    def flow(k, _):
+        @pl.when(k == RING - 2)
+        def _():
+            take(5)
+
+        @pl.when(k == RING)
+        def _():
+            have(5)
+
+        @pl.when(k < 2 * RING)
+        def _():
+            projected(lax.div(k, RING), RING - 1 - lax.rem(k, RING))
+
+        @pl.when(k >= lag)
+        def _():
+            summed(lax.div(k - lag, RING), RING - 1 - lax.rem(k - lag, RING))
+
         return 0
 
-    take(0)
-    take(1)
-    have(0)
-    have(1)
-    lax.fori_loop(0, RING // 2, gated, 0)
-    take(2)
-    have(2)
-    lax.fori_loop(0, RING, projected, 0)
-
-    def mixing(i):
-        wait_for(ret.at[i], ret_recv.at[i])
-        grown = nn(grow, meta[i])
-        return jnp.where(grown[:, :tokens] == place_in, grown[:, tokens:], 0.0).astype(BF)
-
-    def part(i, mixer, n):
-        rows = ret[i, :, :, n : n + wide].astype(F32).reshape(slots, wide).astype(BF)
-        return tn(mixer, rows)
-
-    def reduce(k, _):
-        i = RING - 1 - k
-        mixer = mixing(i)
-
-        @pl.when(i <= 5)
-        def _():
-            wait_for(rsum.at[i + 1], rs_recv.at[i + 1])
-            for n in range(0, width, wide):
-                total = part(i, mixer, n) + rsum[i + 1, :, n : n + wide].astype(F32)
-                stage[i, :, n : n + wide] = total.astype(BF)
-
-        @pl.when(i > 5)
-        def _():
-            for n in range(0, width, wide):
-                stage[i, :, n : n + wide] = part(i, mixer, n).astype(BF)
-
-        @pl.when(i != 2)
-        def _():
-            remote(stage.at[i], rsum.at[i - 1], rs_send.at[i], rs_recv.at[i - 1], up).start()
-
-        @pl.when(i == 2)
-        def _():
-            remote(stage.at[2], rsum.at[1], rs_send.at[2], rs_recv.at[1], across).start()
-
-        return 0
-
-    lax.fori_loop(0, RING - 1, reduce, 0)
-
-    mixer = mixing(0)
-    wait_for(rsum.at[0], rs_recv.at[0])
-    wait_for(rsum.at[1], rs_recv.at[1])
-    for n in range(0, width, wide):
-        near = rsum[0, :, n : n + wide].astype(F32) + rsum[1, :, n : n + wide].astype(F32)
-        out_ref[:, n : n + wide] = (part(0, mixer, n) + near).astype(BF)
+    lax.fori_loop(0, 2 * RING + lag, flow, 0)
 
     for copy in own_copies + meta_copies + cross_copies + sib_copies + diag_copies:
         copy.wait_send()
 
     def drain(i, _):
         wait_for(disp.at[i, pl.ds(0, n_rows - 1)], disp_send.at[i])
-        wait_for(yout.at[i, pl.ds(0, n_rows - 1)], y_send.at[i])
+        for h in range(2):
+            wait_for(yout.at[h, i, pl.ds(0, n_rows - 1)], y_send.at[h, i])
 
         @pl.when((i >= 1) & (i <= 5))
         def _():
@@ -271,7 +289,8 @@
 
         @pl.when(i >= 1)
         def _():
-            wait_for(stage.at[i], rs_send.at[i])
+            for h in range(2):
+                wait_for(stage.at[h, i], rs_send.at[h, i])
 
         return 0
 
@@ -286,23 +305,25 @@
     vmem = pl.BlockSpec(memory_space=pltpu.VMEM)
     hbm = pl.BlockSpec(memory_space=pl.ANY)
     dma = pltpu.SemaphoreType.DMA
+    halves = (2, RING, n_rows, CAP, width // 2)
     scratch = [
         pltpu.VMEM((RING, count, width), BF),
         pltpu.VMEM((RING, n_rows, 2 * count), F32),
         pltpu.VMEM((RING, n_rows, 2 * count), F32),
         pltpu.VMEM(blocks, BF),
         pltpu.VMEM(blocks, BF),
-        pltpu.VMEM(blocks, BF),
-        pltpu.VMEM(blocks, BF),
-        pltpu.VMEM((RING, count, width), BF),
-        pltpu.VMEM((RING, count, width), BF),
+        pltpu.VMEM(halves, BF),
+        pltpu.VMEM(halves, BF),
+        pltpu.VMEM((2, RING, count, width // 2), BF),
+        pltpu.VMEM((2, RING, count, width // 2), BF),
         pltpu.VMEM((4 * quarter, width), BF),
         pltpu.VMEM((4 * quarter, width), BF),
-        pltpu.VMEM((4 * quarter, width), BF),
+        pltpu.VMEM((2, 4 * quarter, width // 2), BF),
         pltpu.VMEM((RING, n_rows * CAP, 4 * quarter), BF),
     ]
-    scratch += [dma((RING,)) for _ in range(10)]
-    scratch += [dma((3,)), dma((18,)), dma((6,)), dma((6,)), dma((6,))]
+    scratch += [dma((RING,)) for _ in range(6)]
+    scratch += [dma((2, RING)) for _ in range(4)]
+    scratch += [dma((6,)), dma((18,)), dma((6,)), dma((6,)), dma((6,))]
     return pl.pallas_call(
         functools.partial(kernel, n_rows),
         out_shape=jax.ShapeDtypeStruct((count, width), BF),

time: 173 us -> 156 us (0.902)
  the two profiles are of different devices: /device:TPU:181 before, /device:TPU:6 now
where the time goes in v3:
time: 156 us; the launch traced here: 155 us
  Pallas kernels  153 us (98%)
  local copies, waits for them, and re-layouts  1.67 us (1%)
    pallas_call x1, Pallas kernels, on_device(): pl.pallas_call(functools.partial(kernel, n_rows), out_shape=jax.ShapeDtyp...  153 us

profile of v3, /device:TPU:6, one launch (start us, length us, event | category | flops | bytes accessed | tf_op | source)
XLA Modules:
  0.0 155.0 jit_solution(899910465381574269)
XLA Ops:
  0.0 153.3 %shard_map.73 = bf16[64,2048]{1,0:T(8,128)(2,1)} custom-call(s32[8,64]{1,0:T(8,128)} %bitcast.3, bf16[8,64]{1,0:T(8,128)(2,1)} %bitcast.4, s32[1,128]{1,0:T(1,128)} %bitcast.5, bf16[64,2048]{1,0:T(8,128)(2,1)} %tok_ref.1, bf16[1,1,1,192,2048]{4,3,2,1,0:T(8,128)(2,1)} %gate_hbm.1, bf16[1,1,1,192,2048]{4,3,2,1,0:T(8,128)(2,1)} %up_hbm.1, ...), custom_call_target="tpu_custom_call" | custom-call | tf_op jit(solution)/shard_map/pallas_call | solution.py:327
  153.3 1.7 %copy.9 = bf16[64,2048]{1,0:T(8,128)(2,1)} copy(bf16[64,2048]{1,0:T(8,128)(2,1)} %shard_map.73) | data formatting | bytes 524288

commit v4 on v3

--- a/solution.py
+++ b/solution.py
@@ -12,6 +12,12 @@
 F32 = jnp.float32
 MESH = pl.DeviceIdType.MESH
 RING = 8
+CUT = 4
+PARTS = (6, 10)
+STRIP = 2
+CUTS = 2
+EARLY = (2, 2, 4, 4, 4)
+LAG = 4
 
 
 def nt(a, b):
@@ -32,7 +38,7 @@
 
 def kernel(
     n_rows, ids_ref, wts_ref, place_ref, tok_ref, gate_hbm, up_hbm, down_hbm, out_ref,
-    tok, meta_out, meta, disp, arr, yout, ret, stage, rsum, gw, uw, dw, hid,
+    tok, meta_out, meta, disp, arr, yout, ret, stage, rsum, gw, uw, dw, hid, mixers, own,
     tok_send, tok_recv, meta_send, meta_recv, disp_send, arr_recv, y_send, ret_recv,
     rs_send, rs_recv, w_local, w_send, w_cross, w_sib, w_diag,
 ):
@@ -83,20 +89,23 @@
     for device in partners:
         pl.semaphore_signal(barrier, inc=1, device_id=device, device_id_type=MESH)
 
-    piece = quarter // 2
-    side = width // 2
+    piece = quarter // CUT
+    spans = tuple(width * n // 16 for n in PARTS)
+    starts = tuple(sum(spans[:h]) for h in range(len(spans)))
+    strip = width * STRIP // 16
+    pieces = 2 * CUT + width // strip
 
     def given(k):
-        if k < 4:
-            return (gate_hbm, up_hbm)[k // 2].at[0, 0, 0, pl.ds(k % 2 * piece, piece)]
-        return down_hbm.at[0, 0, 0, :, pl.ds((k - 4) * side, side)]
+        if k < 2 * CUT:
+            return (gate_hbm, up_hbm)[k // CUT].at[0, 0, 0, pl.ds(k % CUT * piece, piece)]
+        return down_hbm.at[0, 0, 0, :, pl.ds((k - 2 * CUT) * strip, strip)]
 
     def kept(k, place):
-        if k < 4:
-            return (gw, uw)[k // 2].at[pl.ds(place * quarter + k % 2 * piece, piece)]
-        return dw.at[k - 4, pl.ds(place * quarter, quarter)]
-
-    local_copies = [pltpu.make_async_copy(given(k), kept(k, 0), w_local.at[k]) for k in range(6)]
+        if k < 2 * CUT:
+            return (gw, uw)[k // CUT].at[pl.ds(place * quarter + k % CUT * piece, piece)]
+        return dw.at[pl.ds(place * quarter, quarter), pl.ds((k - 2 * CUT) * strip, strip)]
+
+    local_copies = [pltpu.make_async_copy(given(k), kept(k, 0), w_local.at[k]) for k in range(pieces)]
     for copy in local_copies:
         copy.start()
 
@@ -119,10 +128,15 @@
 
     pl.semaphore_wait(barrier, len(partners))
 
-    own_copies = [
-        remote(tok.at[0], tok.at[1], tok_send.at[0], tok_recv.at[1], down),
-        remote(tok.at[0], tok.at[2], tok_send.at[7], tok_recv.at[2], across),
-    ]
+    rows_in = tokens // CUTS
+
+    def block(src, dst, n, send, device):
+        at = pl.ds(n * rows_in, rows_in)
+        return remote(tok.at[src, at], tok.at[dst, at], tok_send.at[send, n], tok_recv.at[dst, n], device)
+
+    own_copies = []
+    for n in range(CUTS):
+        own_copies += [block(0, 1, n, 0, down), block(0, 2, n, 7, across)]
     meta_copies = []
     for slot, (d, part) in enumerate(readers, 1):
         there = lax.rem(g + RING + way * (-d if part else d), RING)
@@ -132,10 +146,11 @@
     for copy in meta_copies + own_copies:
         copy.start()
     meta[0] = meta_out[g]
-    cross_copies = [remote(given(k), kept(k, 2), w_send.at[k], w_cross.at[k], cross) for k in range(6)]
-    sib_copies = [remote(given(k), kept(k, 1), w_send.at[6 + k], w_sib.at[k], sibling) for k in range(6)]
-    diag_copies = [remote(kept(k, 2), kept(k, 3), w_send.at[12 + k], w_diag.at[k], sibling) for k in range(6)]
-    cross_copies[0].start()
+    cross_copies = [remote(given(k), kept(k, 2), w_send.at[k], w_cross.at[k], cross) for k in range(pieces)]
+    sib_copies = [remote(given(k), kept(k, 1), w_send.at[pieces + k], w_sib.at[k], sibling) for k in range(pieces)]
+    diag_copies = [remote(kept(k, 2), kept(k, 3), w_send.at[2 * pieces + k], w_diag.at[k], sibling) for k in range(pieces)]
+    for k in range(EARLY[0]):
+        cross_copies[k].start()
 
     grow = jnp.where(lax.div(iota((slots, n_rows), 0), CAP) == iota((slots, n_rows), 1), 1.0, 0.0)
     place_in = (lax.rem(iota((slots, tokens), 0), CAP) + 1).astype(F32)
@@ -146,25 +161,46 @@
             there = plane(j)
             remote(src.at[there], dst.at[row], send, recv, (there, col)).start()
 
-    wide = min(512, side)
+    wide = min(512, strip)
+    assert all(n % strip == 0 for n in spans)
 
     def dispatch(i, _):
+        def arrive(slot, n):
+            wait_for(tok.at[slot, pl.ds(n * rows_in, rows_in)], tok_recv.at[slot, n])
+
+        @pl.when((i == 1) | (i == 3))
+        def _():
+            for n in range(CUTS):
+                for slot in (i, i + 1):
+                    arrive(slot, n)
+                    block(slot, slot + 2, n, slot, down).start()
+
+        @pl.when(i == 5)
+        def _():
+            for n in range(CUTS):
+                arrive(5, n)
+                block(5, 7, n, 5, down).start()
+
+        @pl.when(i >= 6)
+        def _():
+            for n in range(CUTS):
+                arrive(i, n)
+
         @pl.when(i > 0)
         def _():
-            wait_for(tok.at[i], tok_recv.at[i])
             wait_for(meta.at[i], meta_recv.at[i])
 
-        @pl.when((i >= 1) & (i <= 5))
-        def _():
-            remote(tok.at[i], tok.at[i + 2], tok_send.at[i], tok_recv.at[i + 2], down).start()
-
-        @pl.when(i == 2)
-        def _():
-            cross_copies[1].start()
+        for step in range(1, 5):
+            if EARLY[step] > EARLY[step - 1]:
+
+                @pl.when(i == step)
+                def _():
+                    for k in range(EARLY[step - 1], EARLY[step]):
+                        cross_copies[k].start()
 
         @pl.when(i == 5)
         def _():
-            for copy in cross_copies[2:] + sib_copies:
+            for copy in cross_copies[EARLY[4] :] + sib_copies:
                 copy.start()
 
         grown = nn(grow, meta[i])
@@ -202,95 +238,115 @@
             hid[pl.ds(2 * k, 2), :, h : h + tile] = both.reshape(2, slots, tile)
         return 0
 
-    take(0, 1, 2, 3)
-    have(0, 1, 2, 3)
-    lax.fori_loop(0, RING // 2, gated, 0)
-    take(4)
-    have(4)
-
-    def projected(h, i):
-        for n in range(0, side, wide):
-            y = nn(hid[i], dw[h, :, n : n + wide])
-            yout[h, i, :, :, n : n + wide] = y.reshape(n_rows, CAP, wide).astype(BF)
-        send_rows(yout.at[h, i], ret.at[h, i], y_send.at[h, i], ret_recv.at[h, i])
-
-    def part(h, i, mixer, n):
-        rows = ret[h, i, :, :, n : n + wide].astype(F32).reshape(slots, wide).astype(BF)
-        return tn(mixer, rows)
-
-    def summed(h, i):
-        wait_for(ret.at[h, i], ret_recv.at[h, i])
+    eye = jnp.where(iota((slots, slots), 0) == iota((slots, slots), 1), 1.0, 0.0).astype(BF)
+
+    def mixing(i, _):
         grown = nn(grow, meta[i])
         mixer = jnp.where(grown[:, :tokens] == place_in, grown[:, tokens:], 0.0).astype(BF)
+        mixers[i] = tn(mixer, eye).astype(BF)
+        return 0
+
+    lax.fori_loop(0, RING, mixing, 0)
+
+    take(*range(2 * CUT))
+    have(*range(2 * CUT))
+    lax.fori_loop(0, RING // 2, gated, 0)
+    strips_of = [
+        range(2 * CUT + starts[h] // strip, 2 * CUT + (starts[h] + spans[h]) // strip) for h in range(len(spans))
+    ]
+    take(*strips_of[0])
+    have(*strips_of[0])
+
+    def projected(h, i):
+        for n in range(0, spans[h], wide):
+            y = nn(hid[i], dw[:, starts[h] + n : starts[h] + n + wide])
+            yout[h][i, :, :, n : n + wide] = y.reshape(n_rows, CAP, wide).astype(BF)
+        send_rows(yout[h].at[i], ret[h].at[i], y_send.at[h, i], ret_recv.at[h, i])
+
+    def part(h, i, n):
+        rows = ret[h][i, :, :, n : n + wide].astype(F32).reshape(slots, wide).astype(BF)
+        return nn(mixers[i], rows)
+
+    def summed(h, i):
+        wait_for(ret[h].at[i], ret_recv.at[h, i])
 
         @pl.when((i >= 1) & (i <= 5))
         def _():
-            wait_for(rsum.at[h, i + 1], rs_recv.at[h, i + 1])
-            for n in range(0, side, wide):
-                total = part(h, i, mixer, n) + rsum[h, i + 1, :, n : n + wide].astype(F32)
-                stage[h, i, :, n : n + wide] = total.astype(BF)
+            wait_for(rsum[h].at[i + 1], rs_recv.at[h, i + 1])
+            for n in range(0, spans[h], wide):
+                total = part(h, i, n) + rsum[h][i + 1, :, n : n + wide].astype(F32)
+                stage[h][i, :, n : n + wide] = total.astype(BF)
 
         @pl.when(i > 5)
         def _():
-            for n in range(0, side, wide):
-                stage[h, i, :, n : n + wide] = part(h, i, mixer, n).astype(BF)
+            for n in range(0, spans[h], wide):
+                stage[h][i, :, n : n + wide] = part(h, i, n).astype(BF)
+
+        @pl.when(i == 0)
+        def _():
+            for n in range(0, spans[h], wide):
+                own[:, starts[h] + n : starts[h] + n + wide] = part(h, 0, n)
 
         @pl.when((i >= 1) & (i != 2))
         def _():
-            remote(stage.at[h, i], rsum.at[h, i - 1], rs_send.at[h, i], rs_recv.at[h, i - 1], up).start()
+            remote(stage[h].at[i], rsum[h].at[i - 1], rs_send.at[h, i], rs_recv.at[h, i - 1], up).start()
 
         @pl.when(i == 2)
         def _():
-            remote(stage.at[h, 2], rsum.at[h, 1], rs_send.at[h, 2], rs_recv.at[h, 1], across).start()
-
-        @pl.when(i == 0)
-        def _():
-            wait_for(rsum.at[h, 0], rs_recv.at[h, 0])
-            wait_for(rsum.at[h, 1], rs_recv.at[h, 1])
-            for n in range(0, side, wide):
-                near = rsum[h, 0, :, n : n + wide].astype(F32) + rsum[h, 1, :, n : n + wide].astype(F32)
-                at = pl.multiple_of(h * side + n, wide)
-                out_ref[:, pl.ds(at, wide)] = (part(h, 0, mixer, n) + near).astype(BF)
-
-    lag = 3
+            remote(stage[h].at[2], rsum[h].at[1], rs_send.at[h, 2], rs_recv.at[h, 1], across).start()
 
     def flow(k, _):
-        @pl.when(k == RING - 2)
-        def _():
-            take(5)
-
-        @pl.when(k == RING)
-        def _():
-            have(5)
-
-        @pl.when(k < 2 * RING)
-        def _():
-            projected(lax.div(k, RING), RING - 1 - lax.rem(k, RING))
-
-        @pl.when(k >= lag)
-        def _():
-            summed(lax.div(k - lag, RING), RING - 1 - lax.rem(k - lag, RING))
+        for h in range(1, len(spans)):
+            pace = max(1, RING // 2 // len(strips_of[h]))
+            for n, strip_now in enumerate(strips_of[h]):
+
+                @pl.when(k == RING * h - pace * (len(strips_of[h]) - n))
+                def _(strip_now=strip_now):
+                    take(strip_now)
+
+            @pl.when(k == RING * h)
+            def _():
+                have(*strips_of[h])
+
+        for h in range(len(spans)):
+
+            @pl.when(lax.div(k, RING) == h)
+            def _():
+                projected(h, RING - 1 - lax.rem(k, RING))
+
+        for h in range(len(spans)):
+
+            @pl.when(lax.div(k + RING - LAG, RING) == h + 1)
+            def _():
+                summed(h, RING - 1 - lax.rem(k + RING - LAG, RING))
 
         return 0
 
-    lax.fori_loop(0, 2 * RING + lag, flow, 0)
+    lax.fori_loop(0, len(spans) * RING + LAG, flow, 0)
+
+    for h in range(len(spans)):
+        wait_for(rsum[h].at[0], rs_recv.at[h, 0])
+        wait_for(rsum[h].at[1], rs_recv.at[h, 1])
+        at = pl.ds(starts[h], spans[h])
+        out_ref[:, at] = (own[:, at] + rsum[h][0].astype(F32) + rsum[h][1].astype(F32)).astype(BF)
 
     for copy in own_copies + meta_copies + cross_copies + sib_copies + diag_copies:
         copy.wait_send()
 
     def drain(i, _):
         wait_for(disp.at[i, pl.ds(0, n_rows - 1)], disp_send.at[i])
-        for h in range(2):
-            wait_for(yout.at[h, i, pl.ds(0, n_rows - 1)], y_send.at[h, i])
+        for h in range(len(spans)):
+            wait_for(yout[h].at[i, pl.ds(0, n_rows - 1)], y_send.at[h, i])
 
         @pl.when((i >= 1) & (i <= 5))
         def _():
-            wait_for(tok.at[i], tok_send.at[i])
+            for n in range(CUTS):
+                wait_for(tok.at[i, pl.ds(n * rows_in, rows_in)], tok_send.at[i, n])
 
         @pl.when(i >= 1)
         def _():
-            for h in range(2):
-                wait_for(stage.at[h, i], rs_send.at[h, i])
+            for h in range(len(spans)):
+                wait_for(stage[h].at[i], rs_send.at[h, i])
 
         return 0
 
@@ -305,25 +361,31 @@
     vmem = pl.BlockSpec(memory_space=pltpu.VMEM)
     hbm = pl.BlockSpec(memory_space=pl.ANY)
     dma = pltpu.SemaphoreType.DMA
-    halves = (2, RING, n_rows, CAP, width // 2)
+    spans = tuple(width * n // 16 for n in PARTS)
+    parted = tuple(pltpu.VMEM((RING, n_rows, CAP, n), BF) for n in spans)
+    summing = tuple(pltpu.VMEM((RING, count, n), BF) for n in spans)
     scratch = [
         pltpu.VMEM((RING, count, width), BF),
         pltpu.VMEM((RING, n_rows, 2 * count), F32),
         pltpu.VMEM((RING, n_rows, 2 * count), F32),
         pltpu.VMEM(blocks, BF),
         pltpu.VMEM(blocks, BF),
-        pltpu.VMEM(halves, BF),
-        pltpu.VMEM(halves, BF),
-        pltpu.VMEM((2, RING, count, width // 2), BF),
-        pltpu.VMEM((2, RING, count, width // 2), BF),
+        parted,
+        parted,
+        summing,
+        summing,
         pltpu.VMEM((4 * quarter, width), BF),
         pltpu.VMEM((4 * quarter, width), BF),
-        pltpu.VMEM((2, 4 * quarter, width // 2), BF),
+        pltpu.VMEM((4 * quarter, width), BF),
         pltpu.VMEM((RING, n_rows * CAP, 4 * quarter), BF),
+        pltpu.VMEM((RING, count, n_rows * CAP), BF),
+        pltpu.VMEM((count, width), F32),
     ]
-    scratch += [dma((RING,)) for _ in range(6)]
-    scratch += [dma((2, RING)) for _ in range(4)]
-    scratch += [dma((6,)), dma((18,)), dma((6,)), dma((6,)), dma((6,))]
+    scratch += [dma((RING, CUTS)) for _ in range(2)]
+    scratch += [dma((RING,)) for _ in range(4)]
+    scratch += [dma((len(PARTS), RING)) for _ in range(4)]
+    pieces = 2 * CUT + 16 // STRIP
+    scratch += [dma((pieces,)), dma((3 * pieces,)), dma((pieces,)), dma((pieces,)), dma((pieces,))]
     return pl.pallas_call(
         functools.partial(kernel, n_rows),
         out_shape=jax.ShapeDtypeStruct((count, width), BF),

time: 156 us -> 154 us (0.987)
  no operation moved by 1% of the time
where the time goes in v4:
time: 154 us
  Pallas kernels  153 us (99%)
  local copies, waits for them, and re-layouts  1.67 us (1%)
    pallas_call x1, Pallas kernels, on_device(): pl.pallas_call(functools.partial(kernel, n_rows), out_shape=jax.ShapeDtyp...  153 us

profile of v4, /device:TPU:6, one launch (start us, length us, event | category | flops | bytes accessed | tf_op | source)
XLA Modules:
  0.0 154.2 jit_solution(13224292929750678939)
XLA Ops:
  0.0 152.5 %shard_map.73 = bf16[64,2048]{1,0:T(8,128)(2,1)} custom-call(s32[8,64]{1,0:T(8,128)} %bitcast.3, bf16[8,64]{1,0:T(8,128)(2,1)} %bitcast.4, s32[1,128]{1,0:T(1,128)} %bitcast.5, bf16[64,2048]{1,0:T(8,128)(2,1)} %tok_ref.1, bf16[1,1,1,192,2048]{4,3,2,1,0:T(8,128)(2,1)} %gate_hbm.1, bf16[1,1,1,192,2048]{4,3,2,1,0:T(8,128)(2,1)} %up_hbm.1, ...), custom_call_target="tpu_custom_call" | custom-call | tf_op jit(solution)/shard_map/pallas_call | solution.py:389
  152.5 1.7 %copy.9 = bf16[64,2048]{1,0:T(8,128)(2,1)} copy(bf16[64,2048]{1,0:T(8,128)(2,1)} %shard_map.73) | data formatting | bytes 524288

commit v5 on v4

--- a/solution.py
+++ b/solution.py
@@ -17,7 +17,7 @@
 STRIP = 2
 CUTS = 2
 EARLY = (2, 2, 4, 4, 4)
-LAG = 4
+LAG = 6
 
 
 def nt(a, b):

time: 154 us -> 157 us (1.019); the launches traced: 154 us -> 154 us
  no operation moved by 1% of the time
where the time goes in v5:
time: 157 us; the launch traced here: 154 us
  Pallas kernels  153 us (97%)
  local copies, waits for them, and re-layouts  1.67 us (1%)
    pallas_call x1, Pallas kernels, on_device(): pl.pallas_call(functools.partial(kernel, n_rows), out_shape=jax.ShapeDtyp...  153 us

profile of v5, /device:TPU:6, one launch (start us, length us, event | category | flops | bytes accessed | tf_op | source)
XLA Modules:
  0.0 154.2 jit_solution(11839654085290005624)
XLA Ops:
  0.0 152.5 %shard_map.73 = bf16[64,2048]{1,0:T(8,128)(2,1)} custom-call(s32[8,64]{1,0:T(8,128)} %bitcast.3, bf16[8,64]{1,0:T(8,128)(2,1)} %bitcast.4, s32[1,128]{1,0:T(1,128)} %bitcast.5, bf16[64,2048]{1,0:T(8,128)(2,1)} %tok_ref.1, bf16[1,1,1,192,2048]{4,3,2,1,0:T(8,128)(2,1)} %gate_hbm.1, bf16[1,1,1,192,2048]{4,3,2,1,0:T(8,128)(2,1)} %up_hbm.1, ...), custom_call_target="tpu_custom_call" | custom-call | tf_op jit(solution)/shard_map/pallas_call | solution.py:389
  152.5 1.7 %copy.9 = bf16[64,2048]{1,0:T(8,128)(2,1)} copy(bf16[64,2048]{1,0:T(8,128)(2,1)} %shard_map.73) | data formatting | bytes 524288
